TPU v7x, 128 devices: a whole 4x4x4 slice. The times are simulated.
128 devices in a mesh: section: 8 (over y, x_hi), expert: 16 (over x_lo, z, core).
Axes of the slice: x: 4 (x_hi: 2, x_lo: 2; x = x_hi * 2 + x_lo), y: 4, z: 4, core: 2. Of those that a mesh axis runs over, the one named last changes fastest.
Arguments:
- kv_grads: bfloat16 [8, 2048, 4096], P('section', 'expert'), may hold values from -6 to 6
- kv_weight: bfloat16 [8, 2048, 4096], P('section', 'expert'), may hold values from -0.09375 to 0.09375
- enc_inputs: bfloat16 [8, 2048, 2048], P('section', 'expert')
- enc_gain: float32 [8, 2048], P('section'), may hold values from 0.25 to 1.75
- enc_w1: bfloat16 [8, 2048, 32768], P('section', None, 'expert'), may hold values from -0.125 to 0.125
- enc_w2: bfloat16 [8, 32768, 2048], P('section', 'expert'), may hold values from -0.0625 to 0.0625
- route_ids: int32 [8, 2048, 2], P('section', 'expert'), may hold values from 0 to 3, all different within a row; in each aligned block of 128 rows (0 to 127, 128 to 255, ..., all dimensions but the last counted through in order) at most 68 rows name the same one
- route_probs: float32 [8, 2048, 2], P('section', 'expert'), may hold values from 0.05 to 0.5
- pending_grads: bfloat16 [8, 2048, 2048], P('section', 'expert'), may hold values from -6 to 6
Outputs:
- section_grads: bfloat16 [8, 2048, 2048], P('section', 'expert')
Inputs may be any that keep to these rules, and one draw needn't show every extreme that they name: `route_ids`: within each device's 128 rows (aligned blocks of one section) no expert is chosen more than 68 times, and in some block some expert exactly 68 times; the two choices of a token differ.
All inputs are finite; a program needn't handle non-finite values.
Results may differ from a plain program's by a relative error of at most 0.005.
Values may be sent and summed in bfloat16 or wider, within the bound.
A program may use at most 128 MiB of HBM per device.

v0:
```python
from functools import partial

import jax
import jax.numpy as jnp
from jax import lax
from jax.sharding import PartitionSpec as P

EXPERTS = 4
CAP = 68


EPSILON = 1e-06


def passed_along(block, axis, distance):
    devices = range(lax.axis_size(axis))
    route = [(i - distance, i) for i in devices if i - distance in devices]
    return lax.ppermute(block, axis, route)


def rms_map(inputs, gain):
    values = inputs.astype(jnp.float32)
    factor = lax.rsqrt(jnp.mean(values * values, axis=-1, keepdims=True) + EPSILON)
    return values * factor * gain


def gelu_back(pre_act, upstream):
    return jax.vjp(partial(jax.nn.gelu, approximate=True), pre_act)[1](upstream)[0]


def contract_last(left_side, right_side):
    return lax.dot_general(
        left_side, right_side, (((1,), (1,)), ((), ())), preferred_element_type=jnp.float32
    )


def slot_positions(expert_ids, experts, capacity):
    flat_ids = expert_ids.reshape(-1)
    one_hot = (flat_ids[:, None] == jnp.arange(experts, dtype=jnp.int32)[None, :]).astype(jnp.int32)
    earlier = jnp.cumsum(one_hot, axis=0) - one_hot
    within = jnp.sum(earlier * one_hot, axis=1)
    return (flat_ids * capacity + within).reshape(expert_ids.shape)


def dispatch(positions, first_rows, second_rows, places):
    slot_ids = jnp.arange(places, dtype=jnp.int32)[:, None]
    first_hot = (slot_ids == positions[None, :, 0]).astype(jnp.bfloat16)
    second_hot = (slot_ids == positions[None, :, 1]).astype(jnp.bfloat16)
    summed = jnp.dot(first_hot, first_rows, preferred_element_type=jnp.float32)
    summed = summed + jnp.dot(second_hot, second_rows, preferred_element_type=jnp.float32)
    return summed.astype(jnp.bfloat16)


def body(
    kv_grads, kv_weight, enc_inputs, enc_gain, enc_w1, enc_w2, route_ids, route_probs, pending_grads
):
    sections = lax.axis_size("section")
    expert_count = lax.axis_size("expert")
    sharing = expert_count // EXPERTS
    position = lax.axis_index("section")
    width = enc_inputs.shape[2]
    places = EXPERTS * CAP
    partial_grad = contract_last(
        kv_grads[0], lax.all_gather(kv_weight, "expert", axis=1, tiled=True)[0]
    )
    summed_grad = lax.psum(partial_grad, "section")
    memory_rounded = summed_grad.astype(jnp.bfloat16)
    from_above = passed_along(pending_grads[0], "section", -1)
    incoming = jnp.where(position == sections - 1, memory_rounded, from_above)
    positions = slot_positions(route_ids[0], EXPERTS, CAP)
    normed = rms_map(enc_inputs[0], enc_gain[0]).astype(jnp.bfloat16)

    def spread(slot_rows):
        copies = jnp.broadcast_to(
            slot_rows.reshape(EXPERTS, 1, CAP, width), (EXPERTS, sharing, CAP, width)
        )
        return copies.reshape(expert_count, CAP, width)

    normed_slots = spread(dispatch(positions, normed, normed, places))
    upper_f = incoming.astype(jnp.float32)
    scaled_first = (route_probs[0][:, 0:1] * upper_f).astype(jnp.bfloat16)
    scaled_second = (route_probs[0][:, 1:2] * upper_f).astype(jnp.bfloat16)
    scaled_slots = spread(dispatch(positions, scaled_first, scaled_second, places))
    pre_act = jnp.dot(
        lax.all_to_all(normed_slots, "expert", split_axis=0, concat_axis=0, tiled=True).reshape(
            -1, width
        ),
        enc_w1[0],
        preferred_element_type=jnp.float32,
    )
    scaled_recv = lax.all_to_all(scaled_slots, "expert", split_axis=0, concat_axis=0, tiled=True)
    upstream = contract_last(scaled_recv.reshape(-1, width), enc_w2[0])
    hidden_grad = gelu_back(pre_act, upstream).astype(jnp.bfloat16)
    pieces = contract_last(hidden_grad, enc_w1[0]).astype(jnp.bfloat16)
    returned = lax.all_to_all(
        pieces.reshape(scaled_recv.shape), "expert", split_axis=0, concat_axis=0, tiled=True
    )
    combined = jnp.sum(
        returned.astype(jnp.float32).reshape(EXPERTS, sharing, CAP, width), axis=1
    ).reshape(places, width)
    normed_grad = combined[positions[:, 0]] + combined[positions[:, 1]]
    back_fn = jax.vjp(lambda inner: rms_map(inner, enc_gain[0]), enc_inputs[0].astype(jnp.float32))[
        1
    ]
    result = (upper_f + back_fn(normed_grad)[0]).astype(jnp.bfloat16)
    return result[None]


def solution(mesh):
    return jax.shard_map(
        body,
        mesh=mesh,
        in_specs=(
            P("section", "expert", None),
            P("section", "expert", None),
            P("section", "expert", None),
            P("section", None),
            P("section", None, "expert"),
            P("section", "expert", None),
            P("section", "expert", None),
            P("section", "expert", None),
            P("section", "expert", None),
        ),
        out_specs=P("section", "expert", None),
        check_vma=False,
    )
```

profile of v0, /device:TPU:29, one launch (start us, length us, event | category | flops | bytes accessed | tf_op | source)
XLA Modules:
  0.0 490.3 jit_solution(18127691634589397215)
XLA Ops:
  6.5 0.7 all-gather.2.cloned.1.call-update
  7.3 0.8 copy.17
  8.0 0.1 eq.78
  8.2 0.1 eq.74
  8.3 1.2 reduce-window.6
  9.6 0.1 slice.32
  9.6 0.1 copy.20
  9.8 0.1 copy.21
  9.9 0.1 add_bitcast_fusion
  10.0 0.1 reduce_sum.41
  10.1 0.2 fusion.51
  10.4 1.2 fusion.32
  11.6 1.6 fusion.44
  13.2 1.6 fusion.28
  14.8 0.0 copy-start.4
  14.8 0.3 broadcast_in_dim.14
  15.1 0.0 copy-start.5
  15.1 2.8 broadcast_in_dim.30
  17.8 6.6 %all-to-all-start.1 = ((bf16[16,68,2048]{2,1,0:T(8,128)(2,1)}), bf16[16,68,2048]{2,1,0:T(8,128)(2,1)}, u32[]{:S(2)}, u32[]{:S(2)}) async-start(bf16[16,68,2048]{2,1,0:T(8,128)(2,1)} %bitcast.65), calls=%async_computation.1 | async-start | bytes 9437184 | tf_op jit(solution)/shard_map/all_to_all | solution.py:85
  24.5 2.5 collective-permute-start
  27.0 137.5 %all-gather.2.cloned.1.call-done = bf16[1,2048,4096]{2,1,0:T(8,128)(2,1)} async-done(((bf16[1,128,4096]{2,1,0:T(8,128)(2,1)}), bf16[1,2048,4096]{2,1,0:T(8,128)(2,1)}) %all-gather.2.cloned.1.call-update) | async-done | bytes 16777232 | tf_op jit(solution)/shard_map/all_gather | solution.py:64
  164.5 11.4 %fusion = f32[128,2048]{1,0:T(8,128)S(1)} fusion(bf16[1,2048,4096]{2,1,0:T(8,128)(2,1)} %all-gather.2.cloned.1.call-done, bf16[1,128,4096]{2,1,0:T(8,128)(2,1)S(1)} %copy-done), kind=kOutput, calls=%fused_computation.2 | convolution fusion | flops 2147483648 | bytes 18874368 | tf_op jit(solution)/shard_map/dot_general | solution.py:32
  175.9 72.5 %all-reduce.1 = bf16[128,2048]{1,0:T(8,128)(2,1)S(1)} all-reduce(f32[128,2048]{1,0:T(8,128)S(1)} %fusion), channel_id=1, replica_groups=mesh['section'=8,'expert'=16] {'section'}, use_global_device_ids=true, to_apply=%region_0.0 | all-reduce | flops 262144 | bytes 1572864 | tf_op jit(solution)/shard_map/psum | solution.py:66
  248.4 0.0 collective-permute-done
  248.4 0.1 convert_select_fusion
  248.5 0.0 copy-start.2
  248.5 0.5 fusion.38
  249.1 0.5 fusion.27
  249.6 0.3 broadcast_in_dim.12
  249.9 0.0 all-to-all-done.1
  249.9 2.8 broadcast_in_dim.13
  252.7 17.6 %all-to-all-start = ((bf16[16,68,2048]{2,1,0:T(8,128)(2,1)}), bf16[16,68,2048]{2,1,0:T(8,128)(2,1)}, u32[]{:S(2)}, u32[]{:S(2)}) async-start(bf16[16,68,2048]{2,1,0:T(8,128)(2,1)} %bitcast.66), calls=%async_computation | async-start | bytes 9437184 | tf_op jit(solution)/shard_map/all_to_all | solution.py:91
  270.3 7.1 %reshape.74 = bf16[1088,2048]{1,0:T(8,128)(2,1)} reshape(bf16[16,68,2048]{2,1,0:T(8,128)(2,1)} %all-to-all-done.1) | data formatting | bytes 8912896 | tf_op jit(solution)/shard_map/reshape | solution.py:85
  277.3 55.6 %all-to-all-done = bf16[16,68,2048]{2,1,0:T(8,128)(2,1)} async-done(((bf16[16,68,2048]{2,1,0:T(8,128)(2,1)}), bf16[16,68,2048]{2,1,0:T(8,128)(2,1)}, u32[]{:S(2)}, u32[]{:S(2)}) %all-to-all-start) | async-done | bytes 4456480 | tf_op jit(solution)/shard_map/all_to_all | solution.py:91
  333.0 7.1 %reshape.72 = bf16[1088,2048]{1,0:T(8,128)(2,1)} reshape(bf16[16,68,2048]{2,1,0:T(8,128)(2,1)} %all-to-all-done) | data formatting | bytes 8912896 | tf_op jit(solution)/shard_map/reshape | solution.py:92
  340.0 15.3 %fusion.15 = f32[1088,2048]{1,0:T(8,128)} fusion(bf16[1088,2048]{1,0:T(8,128)(2,1)} %reshape.72, bf16[1,2048,2048]{2,1,0:T(8,128)(2,1)} %param.14), kind=kOutput, calls=%fused_computation.18 | convolution fusion | flops 9126805504 | bytes 21757952 | tf_op jit(solution)/shard_map/dot_general | solution.py:32
  355.3 29.8 %fusion.17 = bf16[1088,2048]{1,0:T(8,128)(2,1)} fusion(bf16[1,2048,2048]{2,1,0:T(8,128)(2,1)} %param.13, f32[1088,2048]{1,0:T(8,128)} %fusion.15, bf16[1088,2048]{1,0:T(8,128)(2,1)} %reshape.74), kind=kOutput, calls=%fused_computation.20 | convolution fusion | flops 18300403712 | bytes 26214400 | tf_op jit(solution)/shard_map/dot_general | solution.py:32
  385.1 7.1 %reshape.75 = bf16[16,68,2048]{2,1,0:T(8,128)(2,1)} reshape(bf16[1088,2048]{1,0:T(8,128)(2,1)} %fusion.17) | data formatting | bytes 8912896 | tf_op jit(solution)/shard_map/reshape | solution.py:96
  392.2 12.1 %all-to-all-start.2 = ((bf16[16,68,2048]{2,1,0:T(8,128)(2,1)}), bf16[16,68,2048]{2,1,0:T(8,128)(2,1)}, u32[]{:S(2)}, u32[]{:S(2)}) async-start(bf16[16,68,2048]{2,1,0:T(8,128)(2,1)} %reshape.75), calls=%async_computation.2 | async-start | bytes 9437184 | tf_op jit(solution)/shard_map/all_to_all | solution.py:95
  404.3 63.5 %all-to-all-done.2 = bf16[16,68,2048]{2,1,0:T(8,128)(2,1)} async-done(((bf16[16,68,2048]{2,1,0:T(8,128)(2,1)}), bf16[16,68,2048]{2,1,0:T(8,128)(2,1)}, u32[]{:S(2)}, u32[]{:S(2)}) %all-to-all-start.2) | async-done | bytes 4456480 | tf_op jit(solution)/shard_map/all_to_all | solution.py:95
  467.8 4.9 %convert_reduce_fusion = f32[4,68,2048]{2,1,0:T(8,128)} fusion(bf16[16,68,2048]{2,1,0:T(8,128)(2,1)} %all-to-all-done.2), kind=kLoop, calls=%fused_computation.6 | loop fusion | flops 3899392 | bytes 6684672 | tf_op jit(solution)/shard_map/reduce_sum | solution.py:98
  472.7 1.8 reshape.78
  474.5 0.0 copy-start.3
  474.5 0.0 copy-start.1
  474.5 2.0 gather_fusion.1
  476.5 1.9 gather_fusion
  478.4 2.0 fusion.35
  480.4 3.0 fusion.37
  (17 shorter events, 0.1 us)
Async XLA Ops:
  6.5 158.0 %copy-start = (bf16[1,128,4096]{2,1,0:T(8,128)(2,1)S(1)}, bf16[1,128,4096]{2,1,0:T(8,128)(2,1)}, u32[]{:S(2)}) copy-start(bf16[1,128,4096]{2,1,0:T(8,128)(2,1)} %param.9) | copy-start | bytes 3145732
  6.5 158.0 %all-gather.2.cloned.1.call-start = ((), (), s32[]{:S(2)}) async-start(), calls=%async_computation.3 | async-start | bytes 17825792 | tf_op jit(solution)/shard_map/all_gather | solution.py:64
  14.8 12.2 %copy-start.4 = (f32[1,128,2]{1,2,0:T(2,128)S(1)}, f32[1,128,2]{1,2,0:T(2,128)}, u32[]{:S(2)}) copy-start(f32[1,128,2]{1,2,0:T(2,128)} %param.16) | copy-start | bytes 3076
  15.1 9.4 %copy-start.5 = (bf16[1,128,2048]{2,1,0:T(8,128)(2,1)S(1)}, bf16[1,128,2048]{2,1,0:T(8,128)(2,1)}, u32[]{:S(2)}) copy-start(bf16[1,128,2048]{2,1,0:T(8,128)(2,1)} %param.17) | copy-start | bytes 1572868
  17.8 232.0 %all-to-all-start.1 = ((bf16[16,68,2048]{2,1,0:T(8,128)(2,1)}), bf16[16,68,2048]{2,1,0:T(8,128)(2,1)}, u32[]{:S(2)}, u32[]{:S(2)}) async-start(bf16[16,68,2048]{2,1,0:T(8,128)(2,1)} %bitcast.65), calls=%async_computation.1 | async-start | bytes 9437184 | tf_op jit(solution)/shard_map/all_to_all | solution.py:85
  24.5 223.9 %collective-permute-start = (bf16[128,2048]{1,0:T(8,128)(2,1)S(1)}, bf16[128,2048]{1,0:T(8,128)(2,1)S(1)}, u32[]{:S(2)}, u32[]{:S(2)}) collective-permute-start(bf16[128,2048]{1,0:T(8,128)(2,1)S(1)} %bitcast.73), channel_id=1, source_target_pairs={{16,0},{32,16},{48,32},{64,48},{80,64},{96,80},{112,96},{17,1},{33... | collective-permute-start | bytes 1572872 | tf_op jit(solution)/shard_map/ppermute | solution.py:18
  248.5 4.1 copy-start.2
  252.7 80.3 %all-to-all-start = ((bf16[16,68,2048]{2,1,0:T(8,128)(2,1)}), bf16[16,68,2048]{2,1,0:T(8,128)(2,1)}, u32[]{:S(2)}, u32[]{:S(2)}) async-start(bf16[16,68,2048]{2,1,0:T(8,128)(2,1)} %bitcast.66), calls=%async_computation | async-start | bytes 9437184 | tf_op jit(solution)/shard_map/all_to_all | solution.py:91
  392.2 75.6 %all-to-all-start.2 = ((bf16[16,68,2048]{2,1,0:T(8,128)(2,1)}), bf16[16,68,2048]{2,1,0:T(8,128)(2,1)}, u32[]{:S(2)}, u32[]{:S(2)}) async-start(bf16[16,68,2048]{2,1,0:T(8,128)(2,1)} %reshape.75), calls=%async_computation.2 | async-start | bytes 9437184 | tf_op jit(solution)/shard_map/all_to_all | solution.py:95
  474.5 3.9 copy-start.3
  474.5 8.9 %copy-start.1 = (bf16[1,128,4096]{2,1,0:T(8,128)(2,1)S(1)}, bf16[1,128,4096]{2,1,0:T(8,128)(2,1)}, u32[]{:S(2)}) copy-start(bf16[1,128,4096]{2,1,0:T(8,128)(2,1)} %param.9) | copy-start | bytes 3145732
Sparse Core Ops, SparseCore 0:
  9.1 155.4 all-gather.1
where the time goes:
time: 499 us; the launch traced here: 490 us
  waiting for transfers between devices  257 us (52%)
  blocking collectives  72.5 us (15%)
  matrix products  60.7 us (12%)
  starting transfers between devices  38.8 us (8%)
  local copies, waits for them, and re-layouts  34.5 us (7%)
  between operations  13.6 us (3%)
  other arithmetic  12.8 us (3%)
    all_gather x1, waiting for transfers between devices, body(): lax.all_gather(kv_weight, 'expert', axis=1, tiled=True)[0]  138 us
    psum x1, blocking collectives, body(): summed_grad = lax.psum(partial_grad, 'section')  72.5 us
    all_to_all x1, waiting for transfers between devices, body(): lax.all_to_all(pieces.reshape(scaled_recv.shape), 'expert', split_axis=0,...  63.5 us
    dot_general x3, matrix products, contract_last(): lax.dot_general(left_side, right_side, (((1,), (1,)), ((), ())), preferre...  56.5 us
    all_to_all x1, waiting for transfers between devices, body(): lax.all_to_all(scaled_slots, 'expert', split_axis=0, concat_axis=0, tiled...  55.6 us
    all_to_all x1, starting transfers between devices, body(): lax.all_to_all(scaled_slots, 'expert', split_axis=0, concat_axis=0, tiled...  17.6 us
    all_to_all x1, starting transfers between devices, body(): lax.all_to_all(pieces.reshape(scaled_recv.shape), 'expert', split_axis=0,...  12.1 us
  transfers between devices with their start and end apart: 5, of which 3 were waited for; matrix products, arithmetic and copies ran while one was open for 6% of the time, Pallas kernels for 0%

commit v1 on v0

v1 whole, which is shorter than its diff:
```python
from functools import partial

import jax
import jax.numpy as jnp
from jax import lax
from jax.experimental import pallas as pl
from jax.experimental.pallas import tpu as pltpu
from jax.sharding import PartitionSpec as P

EXPERTS = 4
CAP = 68
EPSILON = 1e-06

TOK = 128
D = 2048
HALF = D // 2
BLOCK = 144
SIDE = EXPERTS * BLOCK
STEP = 256
LANES = 4
QUARTER = 1024
PLANE = LANES * TOK
CHUNK = 32
PEERS = 16
SECTIONS = 8
BF = jnp.bfloat16
F32 = jnp.float32
MESH = pl.DeviceIdType.MESH


def rms_map(inputs, gain):
    values = inputs.astype(F32)
    factor = lax.rsqrt(jnp.mean(values * values, axis=-1, keepdims=True) + EPSILON)
    return values * factor * gain


def gelu_slope(x):
    scale = 0.7978845608028654
    square = x * x
    t = jnp.tanh(scale * x * (1.0 + 0.044715 * square))
    return 0.5 * (1.0 + t) + 0.5 * x * (1.0 - t * t) * (scale * (1.0 + 3 * 0.044715 * square))


def dot_nt(left, right):
    return lax.dot_general(left, right, (((1,), (1,)), ((), ())), preferred_element_type=F32)


def dot_nn(left, right):
    return jnp.dot(left, right, preferred_element_type=F32)


def rows_of(block):
    return pl.ds(block * BLOCK, BLOCK)


def tick_kernel(
    kvg, kvw, pend, normed, wmat, stmat, w1, w2,
    ng, inc_out,
    W1, W2, GA, GB, QS, QR, QO, PF, RS, FIN, INC, INCX, TK, WX, STX, LN, LS, XN, XS,
    GP, PH, SB, SR, PS, PR, CS, CR, NS, NR,
    loc, ex_s, ex_r, pe_s, inc_r, kv_s, kv_r, zk_s, zk_r, q_s, q_r, rs_s, rs_r, fi_s, ix_s, ix_r,
    st_s, st_r, pa_s, pa_r, sb_s, sb_r, ss_s, ss_r, ps_s, ps_r, cr_s, cr_r, n_s, n_r,
):
    s = lax.axis_index("section")
    e = lax.axis_index("expert")
    xl, z, c = e // 8, (e // 2) % 4, e % 2
    oc, ox = 1 - c, 1 - xl
    zi = z + 1 - 2 * (z % 2)
    zc = 3 - z
    me = s * 2 + xl
    lane = xl * 2 + c

    def dev(x, zz, cc, sec=s):
        return (sec, x * 8 + zz * 2 + cc)

    sib, partner, crossed = dev(xl, z, oc), dev(xl, zi, c), dev(xl, zc, c)
    lanes = [(xl, c), (xl, oc), (ox, c), (ox, oc)]
    group = [None, dev(ox, z, c), dev(xl, zc, c), dev(ox, zc, c)]

    def rc(src, dst, send, recv, where):
        return pltpu.make_async_remote_copy(
            src_ref=src, dst_ref=dst, send_sem=send, recv_sem=recv, device_id=where, device_id_type=MESH
        )

    barrier = pltpu.get_barrier_semaphore()

    def greet(where):
        pl.semaphore_signal(barrier, inc=1, device_id=where, device_id_type=MESH)

    for where in (sib, dev(ox, z, c), dev(ox, z, oc), partner, crossed, dev(ox, zc, c)):
        greet(where)

    def greet_peer(i, _):
        k = (me + i) % PEERS
        greet(dev(k % 2, z, c, k // 2))
        return 0

    lax.fori_loop(1, PEERS, greet_peer, 0)

    @pl.when(s < SECTIONS - 1)
    def _():
        greet(dev(xl, z, 0, s + 1))
        greet(dev(xl, z, 1, s + 1))

    @pl.when(s == SECTIONS - 1)
    def _():
        def greet_source(i, _):
            k = xl * 8 + i

            @pl.when(jnp.logical_not((k == me) & (c == 0)))
            def _():
                greet(dev(k % 2, z, 0, k // 2))

            greet(dev(k % 2, zi, 1, k // 2))
            return 0

        lax.fori_loop(0, PEERS // 2, greet_source, 0)

    zt = z + c * (zi - z)
    lane_t = me // 4
    xt, ct, sub = lane_t // 2, lane_t % 2, me % 4
    own_final = (s == SECTIONS - 1) & (xt == xl) & (zt == z)
    to_self = own_final.astype(jnp.int32)
    pl.semaphore_wait(barrier, 6 + PEERS - 1 + 2 * (s > 0).astype(jnp.int32) + 2 - to_self)

    sends = []

    def lane_rows(x, cc):
        return pl.ds(pl.multiple_of((x * 2 + cc) * TOK, TOK), TOK)

    def lane_cols(x, cc):
        return pl.ds(pl.multiple_of((x * 2 + cc) * QUARTER, QUARTER), QUARTER)

    mine = lane_rows(xl, c)
    kv = []
    for r in range(LANES):
        pair = []
        for i, (source, held) in enumerate(((kvg, GA), (kvw, GB))):
            x, cc = lanes[r]
            part = source.at[:, lane_cols(x, cc)]
            if r == 0:
                pair.append(pltpu.make_async_copy(part, held.at[0, mine], loc.at[i]))
            else:
                pair.append(rc(part, held.at[0, mine], kv_s.at[i, r], kv_r.at[i, r], dev(x, z, cc)))
        kv.append(pair)

    def z_copy(i, r):
        held, where = (GA, partner) if i == 0 else (GB, crossed)
        x, cc = lanes[r]
        rows = lane_rows(x, cc)
        if r == 0:
            source = (kvg, kvw)[i].at[:, lane_cols(xl, c)]
        else:
            source = held.at[0, rows]
        return rc(source, held.at[1, rows], zk_s.at[i, r], zk_r.at[i, r], where)

    zk = [[z_copy(i, r) for i in range(2)] for r in range(LANES)]

    exchange = [
        rc(normed.at[:, pl.ds(pl.multiple_of(oc * HALF, HALF), HALF)],
           TK.at[pl.ds(pl.multiple_of(c * TOK, TOK), TOK)], ex_s.at[0], ex_r.at[0], sib),
        rc(wmat, WX.at[c], ex_s.at[1], ex_r.at[1], sib),
        rc(stmat, STX.at[c], ex_s.at[2], ex_r.at[2], sib),
    ]
    for copy in exchange:
        copy.start()
    for r in (2, 3, 1):
        kv[r][0].start()
        kv[r][1].start()
    for i in range(2):
        zk[0][i].start()
    for i in range(2):
        kv[0][i].start()

    def pend_copy(core):
        return rc(pend.at[:, pl.ds(core * HALF, HALF)], INC.at[pl.ds(pl.multiple_of(c * TOK, TOK), TOK)],
                  pe_s.at[core], inc_r, dev(xl, z, core, s - 1))

    @pl.when(s > 0)
    def _():
        pend_copy(0).start()
        pend_copy(1).start()

    load1 = pltpu.make_async_copy(w1, W1, loc.at[2])
    load2 = pltpu.make_async_copy(w2, W2, loc.at[3])
    load1.start()
    load2.start()

    my_cols = pl.ds(pl.multiple_of(c * HALF, HALF), HALF)
    their_cols = pl.ds(pl.multiple_of(oc * HALF, HALF), HALF)
    my_toks = pl.ds(pl.multiple_of(c * TOK, TOK), TOK)
    their_toks = pl.ds(pl.multiple_of(oc * TOK, TOK), TOK)

    TK[my_toks, :] = normed[:, my_cols]
    WX[c] = wmat[...]
    STX[c] = stmat[...]
    for copy in exchange:
        copy.wait_recv()

    def weights_of(r):
        both = jnp.concatenate([WX[0, rows_of(r), :], WX[1, rows_of(r), :]], axis=1)
        return both, (both > 0).astype(BF)

    def stage1(a, r):
        out, held = ((LN, XN), (LS, XS))[a]
        return rc(out.at[r], held.at[0, c, rows_of(r)], st_s.at[a, r], st_r.at[a, r], group[r])

    def to_partner(a, r):
        held = (XN, XS)[a]
        return rc(held.at[0, c, rows_of(r)], held.at[1, c, rows_of(r)], pa_s.at[a, r], pa_r.at[a, r], partner)

    def to_sib(a, h, r):
        block = (XN, XS)[a].at[h, c, rows_of(r)]
        return rc(block, block, sb_s.at[a, h, r], sb_r.at[a, h, r], sib)

    def from_sib(a, h, r):
        block = (XN, XS)[a].at[h, oc, rows_of(r)]
        return rc(block, block, sb_s.at[a, h, r], sb_r.at[a, h, r], sib)

    def go(copy):
        copy.start()
        sends.append(copy)

    def forward(a, r):
        stage1(a, r).wait_recv()
        go(to_partner(a, r))
        go(to_sib(a, 0, r))

    def hand_over(a, r):
        to_partner(a, r).wait_recv()
        go(to_sib(a, 1, r))

    def take(a, h, blocks):
        for r in blocks:
            from_sib(a, h, r).wait_recv()

    for r in (0, 1, 2, 3):
        _, hot = weights_of(r)
        slots = dot_nn(hot, TK[...]).astype(BF)
        if r == 0:
            XN[0, c, rows_of(0)] = slots
            go(to_partner(0, 0))
            go(to_sib(0, 0, 0))
        else:
            LN[r] = slots
            go(stage1(0, r))

    for r in (1, 2, 3):
        for i in range(2):
            kv[r][i].wait_recv()
            zk[r][i].start()
    forward(0, 1)
    forward(0, 2)
    for i in range(2):
        kv[0][i].wait()
    for r in range(LANES):
        for i in range(2):
            zk[r][i].wait_recv()

    def product(plane, store):
        def tile(j, _):
            cols = pl.ds(pl.multiple_of(j * STEP, STEP), STEP)
            for other in range(2):
                store(other, j, dot_nt(GA[plane], GB[other, cols, :]))
            return 0

        lax.fori_loop(0, PLANE // STEP, tile, 0)

    def keep_theirs(other, j, value):
        QS[:, pl.ds(pl.multiple_of(other * PLANE + j * STEP, STEP), STEP)] = value.astype(BF)

    def keep_mine(other, j, value):
        PF[:, pl.ds(pl.multiple_of(other * PLANE + j * STEP, STEP), STEP)] = value

    product(oc, keep_theirs)
    swap = rc(QS, QR, q_s, q_r, sib)
    swap.start()
    product(c, keep_mine)
    forward(0, 3)
    swap.wait_recv()

    def add_core(j, _):
        rows = pl.ds(pl.multiple_of(j * 64, 64), 64)
        QO[rows, :] = (PF[rows, :] + QR[rows, :].astype(F32)).astype(BF)
        return 0

    lax.fori_loop(0, PLANE // 64, add_core, 0)

    def share(k):
        rows = pl.ds(pl.multiple_of(k * CHUNK, CHUNK), CHUNK)
        return rc(QO.at[rows], RS.at[me], rs_s.at[k], rs_r.at[me], dev(k % 2, z, c, k // 2))

    def share_in(k):
        return rc(RS.at[k], RS.at[k], rs_s.at[k], rs_r.at[k], dev(k % 2, z, c, k // 2))

    def send_share(i, _):
        share((me + i) % PEERS).start()
        return 0

    lax.fori_loop(1, PEERS, send_share, 0)
    RS[me] = QO[pl.ds(pl.multiple_of(me * CHUNK, CHUNK), CHUNK), :]

    def pre_act(h, first, last):
        def tile(j, _):
            cols = pl.ds(pl.multiple_of(j * STEP, STEP), STEP)
            total = dot_nn(XN[h, 0], W1[pl.ds(0, HALF), cols]) + dot_nn(XN[h, 1], W1[pl.ds(HALF, HALF), cols])
            GP[h, :, cols] = gelu_slope(total).astype(BF)
            return 0

        lax.fori_loop(first, last, tile, 0)

    load1.wait()
    hand_over(0, 0)
    hand_over(0, 1)
    take(0, 0, range(4))
    pre_act(0, 0, 8)
    hand_over(0, 2)

    def wait_share(i, _):
        share_in((me + i) % PEERS).wait_recv()
        return 0

    lax.fori_loop(1, PEERS, wait_share, 0)
    total = RS[0].astype(F32)
    for k in range(1, PEERS):
        total = total + RS[k].astype(F32)
    FIN[...] = total.astype(BF)

    def final(p, x, op):
        zz = z if p == 0 else zc
        source = FIN.at[:, pl.ds(p * PLANE + x * STEP, STEP)]
        rows = pl.ds(pl.multiple_of(ct * TOK + sub * CHUNK, CHUNK), CHUNK)
        place = INC.at[rows, pl.ds(pl.multiple_of(zz * STEP, STEP), STEP)]
        away = rc(source, place, fi_s.at[p, x], inc_r, dev(xt, zt, x, SECTIONS - 1))
        at_home = jnp.logical_and(own_final, c == x)

        @pl.when(jnp.logical_not(at_home))
        def _():
            away.start() if op == "start" else away.wait_send()

        if op == "start":
            @pl.when(at_home)
            def _():
                pltpu.make_async_copy(source, place, inc_r).start()

    for p in range(2):
        for x in range(2):
            final(p, x, "start")
    hand_over(0, 3)
    take(0, 1, range(4))
    pre_act(1, 0, 3)
    pltpu.make_async_copy(INC, INC, inc_r).wait()

    inc_swap = rc(INC.at[their_toks], INCX, ix_s, ix_r, sib)
    for r in (0, 1, 2, 3):
        both, hot = weights_of(r)
        slots = (dot_nn(hot, INC[...]) * jnp.sum(both, axis=1, keepdims=True)).astype(BF)
        if r == 0:
            XS[0, c, rows_of(0)] = slots
            go(to_partner(1, 0))
            go(to_sib(1, 0, 0))
        else:
            LS[r] = slots
            go(stage1(1, r))
    go(inc_swap)
    pre_act(1, 3, 6)
    forward(1, 1)
    forward(1, 2)
    hand_over(1, 0)
    pre_act(1, 6, 8)
    forward(1, 3)
    load2.wait()

    def hidden(h, first, rows):
        span = pl.ds(first, rows)

        def tile(j, _):
            cols = pl.ds(pl.multiple_of(j * STEP, STEP), STEP)
            upstream = dot_nt(XS[h, 0, span], W2[cols, pl.ds(0, HALF)]) + dot_nt(XS[h, 1, span], W2[cols, pl.ds(HALF, HALF)])
            GP[h, span, cols] = (upstream * GP[h, span, cols].astype(F32)).astype(BF)
            return 0

        lax.fori_loop(0, D // STEP, tile, 0)

    def pieces(h, first, rows):
        span = pl.ds(first, rows)
        for core, kept in ((oc, SB), (c, PH)):
            def tile(j, _, core=core, kept=kept):
                wide = pl.ds(pl.multiple_of(core * HALF + j * STEP, STEP), STEP)
                cols = pl.ds(pl.multiple_of(j * STEP, STEP), STEP)
                kept[h, span, cols] = dot_nt(GP[h, span, :], W1[wide, :]).astype(BF)
                return 0

            lax.fori_loop(0, HALF // STEP, tile, 0)
            if kept is SB:
                go(core_sum(h, first, rows))

    def core_sum(h, first, rows):
        span = pl.ds(first, rows)
        i = 2 * h + first // (2 * BLOCK)
        return rc(SB.at[h, span], SR.at[h, span], ss_s.at[i], ss_r.at[i], sib)

    def partner_sum(i):
        span = pl.ds(i * 2 * BLOCK, 2 * BLOCK)
        return rc(PS.at[span], PR.at[span], ps_s.at[i], ps_r.at[i], partner)

    def add_cores(i):
        core_sum(1, i * 2 * BLOCK, 2 * BLOCK).wait_recv()

        def some(j, _):
            rows = pl.ds(pl.multiple_of(i * 2 * BLOCK + j * 48, 16), 48)
            PS[rows, :] = (PH[1, rows, :].astype(F32) + SR[1, rows, :].astype(F32)).astype(BF)
            return 0

        lax.fori_loop(0, 6, some, 0)
        go(partner_sum(i))

    take(1, 0, range(4))
    hidden(0, 0, SIDE)
    hand_over(1, 1)
    pieces(0, 0, SIDE)
    hand_over(1, 2)
    take(1, 1, (0, 1))
    hidden(1, 0, 2 * BLOCK)
    pieces(1, 0, 2 * BLOCK)
    hand_over(1, 3)
    add_cores(0)
    take(1, 1, (2, 3))
    hidden(1, 2 * BLOCK, 2 * BLOCK)
    pieces(1, 2 * BLOCK, 2 * BLOCK)
    add_cores(1)

    def give_back(r):
        return rc(CS.at[r], CR.at[r], cr_s.at[r], cr_r.at[r], group[r])

    core_sum(0, 0, SIDE).wait_recv()
    for r in (0, 1, 2, 3):
        if r % 2 == 0:
            partner_sum(r // 2).wait_recv()
        held = CR if r == 0 else CS

        def some(j, _, r=r, held=held):
            rows = pl.ds(pl.multiple_of(r * BLOCK + j * 48, 16), 48)
            value = PH[0, rows, :].astype(F32) + SR[0, rows, :].astype(F32) + PR[rows, :].astype(F32)
            held[r, pl.ds(pl.multiple_of(j * 48, 16), 48), :] = value.astype(BF)
            return 0

        lax.fori_loop(0, 3, some, 0)
        if r > 0:
            go(give_back(r))
    for r in (1, 2, 3):
        give_back(r).wait_recv()

    def gathered(core):
        total = dot_nn(STX[core, :, pl.ds(0, BLOCK)], CR[0])
        for r in range(1, EXPERTS):
            total = total + dot_nn(STX[core, :, pl.ds(r * STEP, BLOCK)], CR[r])
        return total

    NS[...] = gathered(oc)
    last = rc(NS, NR, n_s, n_r, sib)
    go(last)
    ng[:, my_cols] = gathered(c)
    inc_out[:, my_cols] = INC[my_toks, :]
    inc_swap.wait_recv()
    inc_out[:, their_cols] = INCX[...]
    last.wait_recv()
    ng[:, their_cols] = NR[...]

    for copy in exchange:
        copy.wait_send()
    for r in range(LANES):
        for i in range(2):
            if r > 0:
                kv[r][i].wait_send()
            zk[r][i].wait_send()

    @pl.when(s > 0)
    def _():
        pend_copy(0).wait_send()
        pend_copy(1).wait_send()

    swap.wait_send()

    def sent_share(i, _):
        share((me + i) % PEERS).wait_send()
        return 0

    lax.fori_loop(1, PEERS, sent_share, 0)
    for p in range(2):
        for x in range(2):
            final(p, x, "wait")
    for copy in sends:
        copy.wait_send()


def tick(kvg, kvw, pend, normed, wmat, stmat, w1, w2):
    any_place = pl.BlockSpec(memory_space=pl.ANY)
    vmem = pl.BlockSpec(memory_space=pltpu.VMEM)
    dma = pltpu.SemaphoreType.DMA
    V = pltpu.VMEM
    scratch = [
        V((D, D), BF), V((D, D), BF),
        V((2, PLANE, QUARTER), BF), V((2, PLANE, QUARTER), BF),
        V((PLANE, HALF), BF), V((PLANE, HALF), BF), V((PLANE, HALF), BF), V((PLANE, HALF), F32),
        V((PEERS, CHUNK, HALF), BF), V((CHUNK, HALF), BF),
        V((2 * TOK, HALF), BF), V((TOK, HALF), BF), V((2 * TOK, HALF), BF),
        V((2, SIDE, TOK), F32), V((2, TOK, EXPERTS * STEP), BF),
        V((EXPERTS, BLOCK, HALF), BF), V((EXPERTS, BLOCK, HALF), BF),
        V((2, 2, SIDE, HALF), BF), V((2, 2, SIDE, HALF), BF),
        V((2, SIDE, D), BF),
        V((2, SIDE, HALF), BF), V((2, SIDE, HALF), BF), V((2, SIDE, HALF), BF),
        V((SIDE, HALF), BF), V((SIDE, HALF), BF),
        V((EXPERTS, BLOCK, HALF), BF), V((EXPERTS, BLOCK, HALF), BF),
        V((TOK, HALF), F32), V((TOK, HALF), F32),
        dma((4,)), dma((3,)), dma((3,)), dma((2,)), dma, dma((2, 4)), dma((2, 4)), dma((2, 4)), dma((2, 4)),
        dma, dma, dma((PEERS,)), dma((PEERS,)), dma((2, 2)), dma, dma,
        dma((2, 4)), dma((2, 4)), dma((2, 4)), dma((2, 4)), dma((2, 2, 4)), dma((2, 2, 4)),
        dma((4,)), dma((4,)), dma((2,)), dma((2,)), dma((4,)), dma((4,)), dma, dma,
    ]
    return pl.pallas_call(
        tick_kernel,
        out_shape=(jax.ShapeDtypeStruct((TOK, D), F32), jax.ShapeDtypeStruct((TOK, D), BF)),
        in_specs=[any_place] * 3 + [vmem] * 3 + [any_place] * 2,
        out_specs=(vmem, vmem),
        scratch_shapes=scratch,
        compiler_params=pltpu.CompilerParams(
            collective_id=0, has_side_effects=True, vmem_limit_bytes=62 * 1024 * 1024
        ),
        name="tick",
    )(kvg, kvw, pend, normed, wmat, stmat, w1, w2)


def routes(ids, probs):
    e = lax.axis_index("expert")
    xl, zh, c = e // 8, (e // 4) % 2, e % 2
    block = (ids // 2 != xl).astype(jnp.int32) + 2 * (ids % 2 != zh).astype(jnp.int32)
    used = (block[:, :, None] == jnp.arange(EXPERTS)[None, None, :]).any(axis=1)
    order = jnp.arange(TOK)
    earlier = (order[None, :] < order[:, None]).astype(BF)
    ahead = dot_nn(earlier, used.astype(BF)).astype(jnp.int32)
    within = jnp.take_along_axis(ahead, block, axis=1) + c * CAP
    slot = block * BLOCK + within
    place = jnp.arange(SIDE)[:, None]
    wmat = jnp.where(place == slot[None, :, 0], probs[None, :, 0], 0.0)
    wmat = wmat + jnp.where(place == slot[None, :, 1], probs[None, :, 1], 0.0)
    wide = block * STEP + within
    column = jnp.arange(EXPERTS * STEP)[None, :]
    stmat = ((column == wide[:, 0:1]) | (column == wide[:, 1:2])).astype(BF)
    return wmat, stmat


def body(
    kv_grads, kv_weight, enc_inputs, enc_gain, enc_w1, enc_w2, route_ids, route_probs, pending_grads
):
    normed = rms_map(enc_inputs[0], enc_gain[0]).astype(BF)
    wmat, stmat = routes(route_ids[0], route_probs[0])
    normed_grad, incoming = tick(
        kv_grads[0], kv_weight[0], pending_grads[0], normed, wmat, stmat, enc_w1[0], enc_w2[0]
    )
    back_fn = jax.vjp(lambda inner: rms_map(inner, enc_gain[0]), enc_inputs[0].astype(F32))[1]
    result = (incoming.astype(F32) + back_fn(normed_grad)[0]).astype(BF)
    return result[None]


def solution(mesh):
    return jax.shard_map(
        body,
        mesh=mesh,
        in_specs=(
            P("section", "expert", None),
            P("section", "expert", None),
            P("section", "expert", None),
            P("section", None),
            P("section", None, "expert"),
            P("section", "expert", None),
            P("section", "expert", None),
            P("section", "expert", None),
            P("section", "expert", None),
        ),
        out_specs=P("section", "expert", None),
        check_vma=False,
    )
```

time: 499 us -> 184 us (0.37); the launches traced: 490 us -> 184 us
  waiting for transfers between devices: 257 us -> 0 us
  Pallas kernels: 0 us -> 170 us
  blocking collectives: 72.5 us -> 0 us
  matrix products: 60.7 us -> 0.14 us
  starting transfers between devices: 38.8 us -> 0 us
  local copies, waits for them, and re-layouts: 34.5 us -> 4.61 us
  between operations: 13.6 us -> 0.05 us
    pallas_call x0 -> x1, Pallas kernels: none -> 170 us  [tick(): pl.pallas_call(tick_kernel, out_shape=(jax.ShapeDtypeStruct((TOK, D), F32...]
    all_gather x1 -> x0, waiting for transfers between devices: 138 us -> none  [body(): lax.all_gather(kv_weight, 'expert', axis=1, tiled=True)[0]]
    all_to_all x3 -> x0, waiting for transfers between devices: 119 us -> none  [the longest x1 63.5 us: body(): lax.all_to_all(pieces.reshape(scaled_recv.shape), 'expert', split_axis=0,...]
    psum x1 -> x0, blocking collectives: 72.5 us -> none  [body(): summed_grad = lax.psum(partial_grad, 'section')]
    dot_general x7 -> x1, matrix products: 60.7 us -> 0.14 us  [dot_nn(): return jnp.dot(left, right, preferred_element_type=F32)]
    all_to_all x3 -> x0, starting transfers between devices: 36.3 us -> none  [the longest x1 17.6 us: body(): lax.all_to_all(scaled_slots, 'expert', split_axis=0, concat_axis=0, tiled...]
    reshape x4 -> x0, local copies, waits for them, and re-layouts: 23 us -> none  [the longest x1 7.1 us: body(): pieces.reshape(scaled_recv.shape)]
    broadcast_in_dim x4 -> x1, local copies, waits for them, and re-layouts: 6.07 us -> 0.76 us  [routes(): wmat = jnp.where(place == slot[None, :, 0], probs[None, :, 0], 0.0)]
  transfers between devices with their start and end apart: 5 -> 0, of which waited for: 3 -> 0; matrix products, arithmetic and copies ran while one was open for 6% -> 0% of each run, Pallas kernels for 0% -> 0%
where the time goes in v1:
time: 184 us
  Pallas kernels  170 us (92%)
  other arithmetic  8.72 us (5%)
  local copies, waits for them, and re-layouts  4.61 us (3%)
    pallas_call x1, Pallas kernels, tick(): pl.pallas_call(tick_kernel, out_shape=(jax.ShapeDtypeStruct((TOK, D), F32...  170 us

profile of v1, /device:TPU:29, one launch (start us, length us, event | category | flops | bytes accessed | tf_op | source)
XLA Modules:
  0.0 183.9 jit_solution(3492055199515511003)
XLA Ops:
  0.0 1.2 fusion.2
  1.2 0.7 shift-left_or_fusion
  1.9 0.8 slice_bitcast_fusion.1
  2.7 0.1 copy.17
  2.8 0.1 reshape.165
  3.0 0.8 copy.15
  3.7 0.1 select_add_fusion.2
  3.8 0.1 copy.16
  3.9 0.1 convolution_convert_fusion
  4.0 0.0 copy-start
  4.1 0.0 copy-start.1
  4.1 2.4 %gather_fusion = s32[256]{0:T(256)S(1)} fusion(s32[128,4]{0,1:T(4,128)S(1)} %convolution_convert_fusion, s32[256]{0:T(256)S(1)} %reshape.165), kind=kCustom, calls=%fused_computation | custom fusion | bytes 4096 | tf_op jit(solution)/shard_map/jit(take_along_axis)/gather | solution.py:542
  6.5 0.1 reshape.168
  6.6 0.1 multiply_add_fusion
  6.7 0.2 slice_reduce_fusion.1
  6.9 0.9 fusion.8.stmat
  7.8 0.8 select_add_fusion.wmat
  8.6 0.0 copy-done
  8.6 0.0 copy-done.1
  8.6 1.0 fusion.4.normed
  9.5 170.4 %tick.1 = (f32[128,2048]{1,0:T(8,128)}, bf16[128,2048]{1,0:T(8,128)(2,1)}) custom-call(bf16[128,4096]{1,0:T(8,128)(2,1)} %bitcast.60, bf16[128,4096]{1,0:T(8,128)(2,1)} %bitcast.61, bf16[128,2048]{1,0:T(8,128)(2,1)} %bitcast.62, bf16[128,2048]{1,0:T(8,128)(2,1)} %fusion.4.normed, f32[576,128]{1,0:T(8,128)} %select_add_fusion.wmat, ...), custom_call_target="tpu_custom_call" | custom-call | tf_op jit(solution)/shard_map/tick/pallas_call | solution.py:521
  179.9 1.4 fusion.5
  181.4 2.5 %fusion.6 = bf16[1,128,2048]{2,1,0:T(8,128)(2,1)} fusion(f32[128,2048]{1,0:T(8,128)} %get-tuple-element.8, bf16[128,2048]{1,0:T(8,128)(2,1)} %get-tuple-element.7, bf16[1,128,2048]{2,1,0:T(8,128)(2,1)S(1)} %copy-done, f32[128]{0:T(128)S(1)} %multiply_multiply_fusion, f32[2048]{0:T(1024)S(1)} %bitcast.65, f32[128]{0:T(128)S(1)} %fusion.16), kind=kLoop, calls=%fused_computation.13 | loop fusion | flops 2359296 | bytes 2630656 | tf_op jit(solution)/shard_map/broadcast_in_dim | solution.py:563
  (3 shorter events, 0.0 us)
Async XLA Ops:
  4.0 4.5 %copy-start = (bf16[1,128,2048]{2,1,0:T(8,128)(2,1)S(1)}, bf16[1,128,2048]{2,1,0:T(8,128)(2,1)}, u32[]{:S(2)}) copy-start(bf16[1,128,2048]{2,1,0:T(8,128)(2,1)} %param.11) | copy-start | bytes 1572868
  4.1 4.5 %copy-start.1 = (f32[1,2048]{1,0:T(1,128)S(1)}, f32[1,2048]{1,0:T(1,128)}, u32[]{:S(2)}) copy-start(f32[1,2048]{1,0:T(1,128)} %param.12) | copy-start | bytes 24580

commit v2 on v0

v2 whole, which is shorter than its diff:
```python
import jax
import jax.numpy as jnp
from jax import lax
from jax.experimental import pallas as pl
from jax.experimental.pallas import tpu as pltpu
from jax.sharding import PartitionSpec as P

EXPERTS = 4
CAP = 68
EPSILON = 1e-06

TOK = 128
D = 2048
HALF = D // 2
BLOCK = 144
PAIR = 2 * BLOCK
SIDE = EXPERTS * BLOCK
STEP = 256
WIDE = 512
LANES = 4
QUARTER = 1024
PLANE = LANES * TOK
CHUNK = 32
PEERS = 16
SECTIONS = 8
OWN = 0
PART = TOK // 2
BF = jnp.bfloat16
F32 = jnp.float32
MESH = pl.DeviceIdType.MESH


def gelu_slope(x):
    scale = 0.7978845608028654
    square = x * x
    t = jnp.tanh(scale * x * (1.0 + 0.044715 * square))
    return 0.5 * (1.0 + t) + 0.5 * x * (1.0 - t * t) * (scale * (1.0 + 3 * 0.044715 * square))


def dot_nt(left, right):
    return lax.dot_general(left, right, (((1,), (1,)), ((), ())), preferred_element_type=F32)


def dot_nn(left, right):
    return jnp.dot(left, right, preferred_element_type=F32)


def at(start, size, unit=None):
    return pl.ds(pl.multiple_of(start, unit or size), size)


def rows_of(block):
    return pl.ds(block * BLOCK, BLOCK)


def tick_kernel(
    kvg, kvw, pend, enc, gain, ids, probs, w1, w2,
    out,
    W1, W2, GA, GB, QS, QR, QO, PF, RS, FIN, INC, INCX, NB, TK, WX, STX, LN, LS, XN, XS,
    GP, PH, SB, SR, PS, PR, CS, CR, NS, NR, NG,
    loc, ex_s, ex_r, pe_s, inc_r, kv_s, kv_r, zk_s, zk_r, q_s, q_r, rs_s, rs_r, fi_s, ix_s, ix_r,
    st_s, st_r, pa_s, pa_r, sb_s, sb_r, ss_s, ss_r, ps_s, ps_r, cr_s, cr_r, n_s, n_r,
):
    s = lax.axis_index("section")
    e = lax.axis_index("expert")
    xl, z, c = e // 8, (e // 2) % 4, e % 2
    oc, ox = 1 - c, 1 - xl
    zi = z + 1 - 2 * (z % 2)
    zc = 3 - z
    me = s * 2 + xl

    def dev(x, zz, cc, sec=s):
        return (sec, x * 8 + zz * 2 + cc)

    sib, partner, crossed = dev(xl, z, oc), dev(xl, zi, c), dev(xl, zc, c)
    lanes = [(xl, c), (xl, oc), (ox, c), (ox, oc)]
    group = [None, dev(ox, z, c), dev(xl, zc, c), dev(ox, zc, c)]
    my_cols, their_cols = at(c * HALF, HALF), at(oc * HALF, HALF)
    my_toks, their_toks = at(c * TOK, TOK), at(oc * TOK, TOK)

    def rc(src, dst, send, recv, where):
        return pltpu.make_async_remote_copy(
            src_ref=src, dst_ref=dst, send_sem=send, recv_sem=recv, device_id=where, device_id_type=MESH
        )

    sent, due = [], []

    def go(copy, key=None):
        copy.start()
        sent.append(copy)
        if key is not None:
            due.append((key, copy))

    def got(key, copy=None):
        for i, (k, own) in enumerate(due):
            if k == key:
                (copy or own).wait_recv()
                del due[i]
                return

    def gone(done):
        done.wait_send()
        sent[:] = [copy for copy in sent if copy is not done]

    load1 = pltpu.make_async_copy(w1, W1, loc.at[2, 0])
    load2 = pltpu.make_async_copy(w2, W2, loc.at[2, 1])

    barrier = pltpu.get_barrier_semaphore()

    def greet(where):
        pl.semaphore_signal(barrier, inc=1, device_id=where, device_id_type=MESH)

    for where in (sib, dev(ox, z, c), dev(ox, z, oc), partner, crossed, dev(ox, zc, c)):
        greet(where)

    def greet_peer(i, _):
        k = (me + i) % PEERS
        greet(dev(k % 2, z, c, k // 2))
        return 0

    lax.fori_loop(1, PEERS, greet_peer, 0)

    @pl.when(s < SECTIONS - 1)
    def _():
        greet(dev(xl, z, 0, s + 1))
        greet(dev(xl, z, 1, s + 1))

    @pl.when(s == SECTIONS - 1)
    def _():
        def greet_source(i, _):
            k = xl * 8 + i

            @pl.when(jnp.logical_not((k == me) & (c == 0)))
            def _():
                greet(dev(k % 2, z, 0, k // 2))

            greet(dev(k % 2, zi, 1, k // 2))
            return 0

        lax.fori_loop(0, PEERS // 2, greet_source, 0)

    zt = z + c * (zi - z)
    lane_t = me // 4
    xt, ct, sub = lane_t // 2, lane_t % 2, me % 4
    own_final = (s == SECTIONS - 1) & (xt == xl) & (zt == z)

    def lane_cols(x, cc):
        return at((x * 2 + cc) * QUARTER, QUARTER)

    def piece_rows(x, cc, half):
        return at((x * 2 + cc) * TOK + half * PART, PART)

    def kv_piece(i, r, half):
        source, held = ((kvg, GA), (kvw, GB))[i]
        x, cc = lanes[r]
        part = source.at[pl.ds(half * PART, PART), lane_cols(x, cc)]
        target = held.at[0, piece_rows(xl, c, half)]
        if r == 0:
            return pltpu.make_async_copy(part, target, loc.at[i, half])
        return rc(part, target, kv_s.at[i, r, half], kv_r.at[i, r, half], dev(x, z, cc))

    def z_piece(i, r, half):
        held, where = (GA, partner) if i == 0 else (GB, crossed)
        rows = piece_rows(*lanes[r], half)
        if r == 0:
            source = (kvg, kvw)[i].at[pl.ds(half * PART, PART), lane_cols(xl, c)]
        else:
            source = held.at[0, rows]
        return rc(source, held.at[1, rows], zk_s.at[i, r, half], zk_r.at[i, r, half], where)

    pl.semaphore_wait(
        barrier, 6 + PEERS - 1 + 2 * (s > 0).astype(jnp.int32) + 2 - own_final.astype(jnp.int32)
    )
    for i in range(2):
        for half in range(2):
            for r in (2, 3):
                go(kv_piece(i, r, half), ("kv", i, r, half))
    for i in range(2):
        for half in range(2):
            go(kv_piece(i, 1, half), ("kv", i, 1, half))
            go(z_piece(i, 0, half), ("zk", i, 0, half))
    for i in range(2):
        for half in range(2):
            kv_piece(i, 0, half).start()
    load1.start()
    load2.start()

    def norm_rows(j, _):
        rows = at(j * 32, 32)
        values = enc[rows, :].astype(F32)
        factor = lax.rsqrt(jnp.mean(values * values, axis=1, keepdims=True) + EPSILON)
        NB[rows, :] = (values * factor * gain[...]).astype(BF)
        return 0

    lax.fori_loop(0, TOK // 32, norm_rows, 0)
    zh = z // 2
    xd = (ids[...] // 2 != xl).astype(jnp.int32)
    zd = (ids[...] % 2 != zh).astype(jnp.int32)
    block = xd + 2 * zd
    which = lax.broadcasted_iota(jnp.int32, (16, TOK), 0)
    first, second = block[0:1, :] == which, block[1:2, :] == which
    used = (first | second).astype(F32)
    weight = jnp.where(first, probs[0:1, :], 0.0) + jnp.where(second, probs[1:2, :], 0.0)
    row, col = (lax.broadcasted_iota(jnp.int32, (TOK, TOK), i) for i in range(2))
    ahead = dot_nn(used.astype(BF), (row < col).astype(BF)) + (c * CAP).astype(F32)
    rest = jnp.zeros((TOK - 16, TOK), F32)
    ahead_t = jnp.concatenate([ahead, rest], axis=0).T
    used_t = jnp.concatenate([used, rest], axis=0).T
    slot = lax.broadcasted_iota(jnp.int32, (BLOCK, TOK), 0).astype(F32)
    column = lax.broadcasted_iota(jnp.int32, (TOK, STEP), 1).astype(F32)
    for p in range(EXPERTS):
        WX[c, rows_of(p), :] = jnp.where(slot == ahead[p:p + 1, :], weight[p:p + 1, :], 0.0)
        hit = jnp.where(column == ahead_t[:, p:p + 1], used_t[:, p:p + 1], 0.0)
        STX[c, :, pl.ds(p * STEP, STEP)] = hit.astype(BF)

    exchange = [
        rc(NB.at[:, their_cols], TK.at[my_toks], ex_s.at[0], ex_r.at[0], sib),
        rc(WX.at[c], WX.at[c], ex_s.at[1], ex_r.at[1], sib),
        rc(STX.at[c], STX.at[c], ex_s.at[2], ex_r.at[2], sib),
    ]
    for i in range(3):
        go(exchange[i], ("ex", i))
    TK[my_toks, :] = NB[:, my_cols]

    def kv_forward(i, r, half):
        got(("kv", i, r, half))
        go(z_piece(i, r, half), ("zk", i, r, half))

    for i in range(2):
        for half in range(2):
            kv_forward(i, 1, half)
    for r in (2, 3):
        kv_forward(0, r, 0)

    for i in range(3):
        got(("ex", i))

    def weights_of(p):
        both = jnp.concatenate([WX[0, rows_of(p), :], WX[1, rows_of(p), :]], axis=1)
        return both, (both > 0).astype(BF)

    for p in range(EXPERTS):
        _, hot = weights_of(p)
        slots = dot_nn(hot, TK[...]).astype(BF)
        if p == OWN:
            XN[0, c, rows_of(p)] = slots
        else:
            LN[p] = slots

    def stage1(a, p):
        source, held = ((LN, XN), (LS, XS))[a]
        return rc(source.at[p], held.at[0, c, rows_of(p)], st_s.at[a, p], st_r.at[a, p], group[p])

    def to_partner(a, p):
        held = (XN, XS)[a]
        return rc(held.at[0, c, rows_of(p)], held.at[1, c, rows_of(p)], pa_s.at[a, p], pa_r.at[a, p], partner)

    def to_sib(a, h, p):
        part = (XN, XS)[a].at[h, c, rows_of(p)]
        return rc(part, part, sb_s.at[a, h, p], sb_r.at[a, h, p], sib)

    def send_out(a, p):
        copy = stage1(a, p)
        go(copy, ("st", a, p))
        return copy

    def pass_on(a, p):
        go(to_partner(a, p), ("pa", a, p))
        go(to_sib(a, 0, p), ("sb", a, 0, p))

    def forward(a, p):
        got(("st", a, p))
        pass_on(a, p)

    def hand_over(a, p):
        got(("pa", a, p))
        go(to_sib(a, 1, p), ("sb", a, 1, p))

    def take(a, h, blocks):
        for p in blocks:
            part = (XN, XS)[a].at[h, oc, rows_of(p)]
            got(("sb", a, h, p), rc(part, part, sb_s.at[a, h, p], sb_r.at[a, h, p], sib))

    send_out(0, 1)
    send_out(0, 2)
    for r in (2, 3):
        kv_forward(0, r, 1)
    pass_on(0, OWN)
    for half in range(2):
        for r in (2, 3):
            kv_forward(1, r, half)
    send_out(0, 3)

    def pend_copy(core):
        return rc(pend.at[:, pl.ds(core * HALF, HALF)], INC.at[my_toks], pe_s.at[core], inc_r, dev(xl, z, core, s - 1))

    for i in range(2):
        for half in range(2):
            kv_piece(i, 0, half).wait()
            for r in range(LANES):
                if i == 0:
                    got(("zk", 0, r, half))

    def product(plane, p, store):
        for j in range(2):
            cols = pl.ds(j * STEP, STEP)
            store(p, cols, dot_nt(GA[plane], GB[p, cols, :]))

    def keep_theirs(p, cols, value):
        QS[p, :, cols] = value.astype(BF)

    def keep_mine(p, cols, value):
        PF[p, :, cols] = value

    def share(p, k):
        return rc(QO.at[p, at(k * CHUNK, CHUNK)], RS.at[p, me], rs_s.at[p, k], rs_r.at[p, me], dev(k % 2, z, c, k // 2))

    def share_in(p, k):
        return rc(RS.at[p, k], RS.at[p, k], rs_s.at[p, k], rs_r.at[p, k], dev(k % 2, z, c, k // 2))

    def spread(p):
        got(("swap", p))

        def add_core(j, _):
            rows = at(j * 64, 64)
            QO[p, rows, :] = (PF[p, rows, :] + QR[p, rows, :].astype(F32)).astype(BF)
            return 0

        lax.fori_loop(0, PLANE // 64, add_core, 0)

        def send_share(i, _):
            share(p, (me + i) % PEERS).start()
            return 0

        lax.fori_loop(1, PEERS, send_share, 0)
        RS[p, me] = QO[p, at(me * CHUNK, CHUNK), :]

    def half_product(p):
        product(oc, p, keep_theirs)
        go(rc(QS.at[p], QR.at[p], q_s.at[p], q_r.at[p], sib), ("swap", p))
        product(c, p, keep_mine)

    half_product(0)
    spread(0)
    for half in range(2):
        for r in range(LANES):
            got(("zk", 1, r, half))
    half_product(1)
    forward(0, 1)
    forward(0, 2)
    spread(1)

    @pl.when(s > 0)
    def _():
        pend_copy(0).start()
        pend_copy(1).start()

    def pre_act(h, first, rows):
        span = pl.ds(first, rows)

        def tile(j, _):
            cols = at(j * WIDE, WIDE)
            total = dot_nn(XN[h, 0, span], W1[pl.ds(0, HALF), cols]) + dot_nn(XN[h, 1, span], W1[pl.ds(HALF, HALF), cols])
            GP[h, span, cols] = gelu_slope(total).astype(BF)
            return 0

        lax.fori_loop(0, D // WIDE, tile, 0)

    load1.wait()
    take(0, 0, (0, 1))
    pre_act(0, 0, PAIR)
    forward(0, 3)

    def settle(p):
        def wait_share(i, _):
            share_in(p, (me + i) % PEERS).wait_recv()
            return 0

        lax.fori_loop(1, PEERS, wait_share, 0)
        total = RS[p, 0].astype(F32)
        for k in range(1, PEERS):
            total = total + RS[p, k].astype(F32)
        FIN[p] = total.astype(BF)
        for x in range(2):
            final(p, x, "start")

    def final(p, x, op):
        zz = z if p == 0 else zc
        source = FIN.at[p, :, pl.ds(x * STEP, STEP)]
        target = INC.at[at(ct * TOK + sub * CHUNK, CHUNK), at(zz * STEP, STEP)]
        away = rc(source, target, fi_s.at[p, x], inc_r, dev(xt, zt, x, SECTIONS - 1))
        at_home = jnp.logical_and(own_final, c == x)

        @pl.when(jnp.logical_not(at_home))
        def _():
            away.start() if op == "start" else away.wait_send()

        if op == "start":
            @pl.when(at_home)
            def _():
                pltpu.make_async_copy(source, target, inc_r).start()

    settle(0)
    hand_over(0, 0)
    hand_over(0, 1)
    settle(1)
    take(0, 0, (2, 3))
    pre_act(0, PAIR, PAIR)
    hand_over(0, 2)
    pltpu.make_async_copy(INC, INC, inc_r).wait()

    def scaled(p):
        both, hot = weights_of(p)
        return (dot_nn(hot, INC[...]) * jnp.sum(both, axis=1, keepdims=True)).astype(BF)

    XS[0, c, rows_of(OWN)] = scaled(OWN)
    pass_on(1, OWN)
    LS[1] = scaled(1)
    leaving = send_out(1, 1)
    LS[2] = scaled(2)
    send_out(1, 2)
    LS[3] = scaled(3)
    go(rc(INC.at[their_toks], INCX, ix_s, ix_r, sib), "inc")
    take(0, 1, (0, 1))
    pre_act(1, 0, PAIR)
    gone(leaving)
    send_out(1, 3)
    forward(1, 1)
    forward(1, 2)
    hand_over(0, 3)
    take(0, 1, (2, 3))
    pre_act(1, PAIR, PAIR)
    hand_over(1, 0)
    load2.wait()

    def hidden(h, first, rows):
        span = pl.ds(first, rows)

        def tile(j, _):
            cols = at(j * WIDE, WIDE)
            upstream = dot_nt(XS[h, 0, span], W2[cols, pl.ds(0, HALF)]) + dot_nt(XS[h, 1, span], W2[cols, pl.ds(HALF, HALF)])
            GP[h, span, cols] = (upstream * GP[h, span, cols].astype(F32)).astype(BF)
            return 0

        lax.fori_loop(0, D // WIDE, tile, 0)

    def pieces(h, first, rows):
        span = pl.ds(first, rows)
        for core, kept in ((oc, SB), (c, PH)):
            def tile(j, _, core=core, kept=kept):
                cols = at(j * WIDE, WIDE)
                kept[h, span, cols] = dot_nt(GP[h, span, :], W1[at(core * HALF + j * WIDE, WIDE), :]).astype(BF)
                return 0

            lax.fori_loop(0, HALF // WIDE, tile, 0)
            if kept is SB:
                i = 2 * h + first // PAIR
                go(rc(SB.at[h, span], SR.at[h, span], ss_s.at[i], ss_r.at[i], sib), ("ss", i))

    def partner_sum(p):
        return rc(PS.at[rows_of(p)], PR.at[rows_of(p)], ps_s.at[p], ps_r.at[p], partner)

    def add_cores(i, blocks):
        got(("ss", 2 + i))
        for p in blocks:
            def some(j, _, p=p):
                rows = at(p * BLOCK + j * 48, 48, 16)
                PS[rows, :] = (PH[1, rows, :].astype(F32) + SR[1, rows, :].astype(F32)).astype(BF)
                return 0

            lax.fori_loop(0, 3, some, 0)
            go(partner_sum(p), ("ps", p))

    take(1, 0, (0, 1))
    hidden(0, 0, PAIR)
    forward(1, 3)
    pieces(0, 0, PAIR)
    hand_over(1, 1)
    take(1, 1, (0, 1))
    hidden(1, 0, PAIR)
    hand_over(1, 2)
    pieces(1, 0, PAIR)
    add_cores(0, (1, 0))
    hand_over(1, 3)
    take(1, 1, (2, 3))
    hidden(1, PAIR, PAIR)
    pieces(1, PAIR, PAIR)
    add_cores(1, (3, 2))
    take(1, 0, (2, 3))
    hidden(0, PAIR, PAIR)

    def complete(p):
        got(("ps", p))
        held = CR if p == OWN else CS

        def some(j, _):
            rows = at(p * BLOCK + j * 48, 48, 16)
            value = PH[0, rows, :].astype(F32) + SR[0, rows, :].astype(F32) + PR[rows, :].astype(F32)
            held[p, at(j * 48, 48, 16), :] = value.astype(BF)
            return 0

        lax.fori_loop(0, 3, some, 0)
        if p != OWN:
            go(rc(CS.at[p], CR.at[p], cr_s.at[p], cr_r.at[p], group[p]), ("cr", p))

    def gathered(core, p):
        return dot_nn(STX[core, :, pl.ds(p * STEP, BLOCK)], CR[p])

    got(("ss", 0))
    complete(1)
    pieces(0, PAIR, PAIR)
    complete(OWN)
    got(("ss", 1))
    complete(3)
    got(("cr", 1))
    NS[...] = gathered(oc, OWN) + gathered(oc, 1)
    NG[...] = gathered(c, OWN) + gathered(c, 1)
    complete(2)
    got(("cr", 3))
    NS[...] = NS[...] + gathered(oc, 3)
    NG[...] = NG[...] + gathered(c, 3)
    got(("cr", 2))
    NS[...] = NS[...] + gathered(oc, 2)
    go(rc(NS, NR, n_s, n_r, sib), "last")
    NG[...] = NG[...] + gathered(c, 2)
    got("inc")
    got("last")

    def finish(j, _):
        rows = at(j * 32, 32)
        mine_x, their_x = enc[rows, my_cols].astype(F32), enc[rows, their_cols].astype(F32)
        mine_g, their_g = NG[rows, :] * gain[:, my_cols], NR[rows, :] * gain[:, their_cols]
        power = jnp.sum(mine_x * mine_x, axis=1, keepdims=True) + jnp.sum(their_x * their_x, axis=1, keepdims=True)
        factor = lax.rsqrt(power * (1.0 / D) + EPSILON)
        along = jnp.sum(mine_g * mine_x, axis=1, keepdims=True) + jnp.sum(their_g * their_x, axis=1, keepdims=True)
        pull = along * factor * factor * factor * (1.0 / D)
        incoming = INC[at(c * TOK + j * 32, 32), :].astype(F32)
        out[rows, my_cols] = (incoming + mine_g * factor - mine_x * pull).astype(BF)
        out[rows, their_cols] = (INCX[rows, :].astype(F32) + their_g * factor - their_x * pull).astype(BF)
        return 0

    lax.fori_loop(0, TOK // 32, finish, 0)

    @pl.when(s > 0)
    def _():
        pend_copy(0).wait_send()
        pend_copy(1).wait_send()

    def sent_share(i, _):
        for p in range(2):
            share(p, (me + i) % PEERS).wait_send()
        return 0

    lax.fori_loop(1, PEERS, sent_share, 0)
    for p in range(2):
        for x in range(2):
            final(p, x, "wait")
    for copy in sent:
        copy.wait_send()


def tick(kvg, kvw, pend, enc, gain, ids, probs, w1, w2):
    any_place = pl.BlockSpec(memory_space=pl.ANY)
    vmem = pl.BlockSpec(memory_space=pltpu.VMEM)
    dma = pltpu.SemaphoreType.DMA
    V = pltpu.VMEM
    scratch = [
        V((D, D), BF), V((D, D), BF),
        V((2, PLANE, QUARTER), BF), V((2, PLANE, QUARTER), BF),
        V((2, PLANE, PLANE), BF), V((2, PLANE, PLANE), BF), V((2, PLANE, PLANE), BF), V((2, PLANE, PLANE), F32),
        V((2, PEERS, CHUNK, PLANE), BF), V((2, CHUNK, PLANE), BF),
        V((2 * TOK, HALF), BF), V((TOK, HALF), BF), V((TOK, D), BF), V((2 * TOK, HALF), BF),
        V((2, SIDE, TOK), F32), V((2, TOK, EXPERTS * STEP), BF),
        V((EXPERTS, BLOCK, HALF), BF), V((EXPERTS, BLOCK, HALF), BF),
        V((2, 2, SIDE, HALF), BF), V((2, 2, SIDE, HALF), BF),
        V((2, SIDE, D), BF),
        V((2, SIDE, HALF), BF), V((2, SIDE, HALF), BF), V((2, SIDE, HALF), BF),
        V((SIDE, HALF), BF), V((SIDE, HALF), BF),
        V((EXPERTS, BLOCK, HALF), BF), V((EXPERTS, BLOCK, HALF), BF),
        V((TOK, HALF), F32), V((TOK, HALF), F32), V((TOK, HALF), F32),
        dma((3, 2)), dma((3,)), dma((3,)), dma((2,)), dma, dma((2, 4, 2)), dma((2, 4, 2)), dma((2, 4, 2)), dma((2, 4, 2)),
        dma((2,)), dma((2,)), dma((2, PEERS)), dma((2, PEERS)), dma((2, 2)), dma, dma,
        dma((2, 4)), dma((2, 4)), dma((2, 4)), dma((2, 4)), dma((2, 2, 4)), dma((2, 2, 4)),
        dma((4,)), dma((4,)), dma((4,)), dma((4,)), dma((4,)), dma((4,)), dma, dma,
    ]
    return pl.pallas_call(
        tick_kernel,
        out_shape=jax.ShapeDtypeStruct((TOK, D), BF),
        in_specs=[any_place] * 3 + [vmem] * 4 + [any_place] * 2,
        out_specs=vmem,
        scratch_shapes=scratch,
        compiler_params=pltpu.CompilerParams(
            collective_id=0, has_side_effects=True, vmem_limit_bytes=62 * 1024 * 1024
        ),
        name="tick",
    )(kvg, kvw, pend, enc, gain, ids, probs, w1, w2)


def body(
    kv_grads, kv_weight, enc_inputs, enc_gain, enc_w1, enc_w2, route_ids, route_probs, pending_grads
):
    return tick(
        kv_grads[0], kv_weight[0], pending_grads[0], enc_inputs[0], enc_gain, route_ids[0].T, route_probs[0].T,
        enc_w1[0], enc_w2[0],
    )[None]


def solution(mesh):
    return jax.shard_map(
        body,
        mesh=mesh,
        in_specs=(
            P("section", "expert", None),
            P("section", "expert", None),
            P("section", "expert", None),
            P("section", None),
            P("section", None, "expert"),
            P("section", "expert", None),
            P("section", "expert", None),
            P("section", "expert", None),
            P("section", "expert", None),
        ),
        out_specs=P("section", "expert", None),
        check_vma=False,
    )
```

time: 499 us -> 152 us (0.30); the launches traced: 490 us -> 152 us
  waiting for transfers between devices: 257 us -> 0 us
  Pallas kernels: 0 us -> 150 us
  blocking collectives: 72.5 us -> 0 us
  matrix products: 60.7 us -> 0 us
  starting transfers between devices: 38.8 us -> 0 us
  local copies, waits for them, and re-layouts: 34.5 us -> 1.88 us
  between operations: 13.6 us -> 0.01 us
  other arithmetic: 12.8 us -> 0 us
    pallas_call x0 -> x1, Pallas kernels: none -> 150 us  [tick(): pl.pallas_call(tick_kernel, out_shape=jax.ShapeDtypeStruct((TOK, D), BF),...]
    all_gather x1 -> x0, waiting for transfers between devices: 138 us -> none  [body(): lax.all_gather(kv_weight, 'expert', axis=1, tiled=True)[0]]
    all_to_all x3 -> x0, waiting for transfers between devices: 119 us -> none  [the longest x1 63.5 us: body(): lax.all_to_all(pieces.reshape(scaled_recv.shape), 'expert', split_axis=0,...]
    psum x1 -> x0, blocking collectives: 72.5 us -> none  [body(): summed_grad = lax.psum(partial_grad, 'section')]
    dot_general x7 -> x0, matrix products: 60.7 us -> none  [the longest x3 56.5 us: contract_last(): lax.dot_general(left_side, right_side, (((1,), (1,)), ((), ())), preferre...]
    all_to_all x3 -> x0, starting transfers between devices: 36.3 us -> none  [the longest x1 17.6 us: body(): lax.all_to_all(scaled_slots, 'expert', split_axis=0, concat_axis=0, tiled...]
    reshape x4 -> x0, local copies, waits for them, and re-layouts: 23 us -> none  [the longest x1 7.1 us: body(): pieces.reshape(scaled_recv.shape)]
    reduce_sum x4 -> x0, other arithmetic: 8.13 us -> none  [the longest x1 4.93 us: body(): jnp.sum(returned.astype(jnp.float32).reshape(EXPERTS, sharing, CAP, width...]
  transfers between devices with their start and end apart: 5 -> 0, of which waited for: 3 -> 0; matrix products, arithmetic and copies ran while one was open for 6% -> 0% of each run, Pallas kernels for 0% -> 0%
where the time goes in v2:
time: 152 us
  Pallas kernels  150 us (99%)
  local copies, waits for them, and re-layouts  1.88 us (1%)
    pallas_call x1, Pallas kernels, tick(): pl.pallas_call(tick_kernel, out_shape=jax.ShapeDtypeStruct((TOK, D), BF),...  150 us

profile of v2, /device:TPU:29, one launch (start us, length us, event | category | flops | bytes accessed | tf_op | source)
XLA Modules:
  0.0 151.9 jit_solution(8264064608887694790)
XLA Ops:
  0.0 150.0 %tick.1 = bf16[128,2048]{1,0:T(8,128)(2,1)} custom-call(bf16[128,4096]{1,0:T(8,128)(2,1)} %bitcast.16, bf16[128,4096]{1,0:T(8,128)(2,1)} %bitcast.17, bf16[128,2048]{1,0:T(8,128)(2,1)} %bitcast.18, bf16[128,2048]{1,0:T(8,128)(2,1)} %bitcast.19, f32[1,2048]{1,0:T(1,128)} %gain.1, s32[2,128]{1,0:T(2,128)} %bitcast.20, f32[2,128]{1,0:T(2,128)} %bitcast.21, ...), custom_call_target="tpu_custom_call" | custom-call | tf_op jit(solution)/shard_map/tick/pallas_call | solution.py:586
  150.0 1.9 %copy.11 = bf16[1,128,2048]{2,1,0:T(8,128)(2,1)} copy(bf16[1,128,2048]{2,1,0:T(8,128)(2,1)} %bitcast.15) | data formatting | bytes 1048576

commit v3 on v2

--- a/solution.py
+++ b/solution.py
@@ -128,7 +128,7 @@
     @pl.when(s == SECTIONS - 1)
     def _():
         def greet_source(i, _):
-            k = xl * 8 + i
+            k = i * 2 + xl
 
             @pl.when(jnp.logical_not((k == me) & (c == 0)))
             def _():
@@ -140,8 +140,7 @@
         lax.fori_loop(0, PEERS // 2, greet_source, 0)
 
     zt = z + c * (zi - z)
-    lane_t = me // 4
-    xt, ct, sub = lane_t // 2, lane_t % 2, me % 4
+    xt, ct, sub = xl, s // 4, s % 4
     own_final = (s == SECTIONS - 1) & (xt == xl) & (zt == z)
 
     def lane_cols(x, cc):
@@ -286,10 +285,11 @@
     for r in (2, 3):
         kv_forward(0, r, 1)
     pass_on(0, OWN)
-    for half in range(2):
-        for r in (2, 3):
-            kv_forward(1, r, half)
-    send_out(0, 3)
+    for r in (2, 3):
+        kv_forward(1, r, 0)
+    forward(0, 2)
+    for r in (2, 3):
+        kv_forward(1, r, 1)
 
     def pend_copy(core):
         return rc(pend.at[:, pl.ds(core * HALF, HALF)], INC.at[my_toks], pe_s.at[core], inc_r, dev(xl, z, core, s - 1))
@@ -312,8 +312,11 @@
     def keep_mine(p, cols, value):
         PF[p, :, cols] = value
 
+    def chunk_of(k):
+        return at((k % 2 * 8 + k // 2) * CHUNK, CHUNK)
+
     def share(p, k):
-        return rc(QO.at[p, at(k * CHUNK, CHUNK)], RS.at[p, me], rs_s.at[p, k], rs_r.at[p, me], dev(k % 2, z, c, k // 2))
+        return rc(QO.at[p, chunk_of(k)], RS.at[p, me], rs_s.at[p, k], rs_r.at[p, me], dev(k % 2, z, c, k // 2))
 
     def share_in(p, k):
         return rc(RS.at[p, k], RS.at[p, k], rs_s.at[p, k], rs_r.at[p, k], dev(k % 2, z, c, k // 2))
@@ -333,7 +336,7 @@
             return 0
 
         lax.fori_loop(1, PEERS, send_share, 0)
-        RS[p, me] = QO[p, at(me * CHUNK, CHUNK), :]
+        RS[p, me] = QO[p, chunk_of(me), :]
 
     def half_product(p):
         product(oc, p, keep_theirs)
@@ -342,12 +345,12 @@
 
     half_product(0)
     spread(0)
+    forward(0, 1)
+    send_out(0, 3)
     for half in range(2):
         for r in range(LANES):
             got(("zk", 1, r, half))
     half_product(1)
-    forward(0, 1)
-    forward(0, 2)
     spread(1)
 
     @pl.when(s > 0)
@@ -367,9 +370,6 @@
         lax.fori_loop(0, D // WIDE, tile, 0)
 
     load1.wait()
-    take(0, 0, (0, 1))
-    pre_act(0, 0, PAIR)
-    forward(0, 3)
 
     def settle(p):
         def wait_share(i, _):
@@ -401,12 +401,20 @@
                 pltpu.make_async_copy(source, target, inc_r).start()
 
     settle(0)
+    forward(0, 3)
+    take(0, 0, (0, 1))
+    pre_act(0, 0, PAIR)
     hand_over(0, 0)
-    hand_over(0, 1)
-    settle(1)
+    hand_over(0, 2)
     take(0, 0, (2, 3))
     pre_act(0, PAIR, PAIR)
-    hand_over(0, 2)
+    settle(1)
+    hand_over(0, 1)
+    take(0, 1, (0, 1))
+    pre_act(1, 0, PAIR)
+    hand_over(0, 3)
+    take(0, 1, (2, 3))
+    pre_act(1, PAIR, PAIR)
     pltpu.make_async_copy(INC, INC, inc_r).wait()
 
     def scaled(p):
@@ -421,15 +429,10 @@
     send_out(1, 2)
     LS[3] = scaled(3)
     go(rc(INC.at[their_toks], INCX, ix_s, ix_r, sib), "inc")
-    take(0, 1, (0, 1))
-    pre_act(1, 0, PAIR)
     gone(leaving)
     send_out(1, 3)
     forward(1, 1)
     forward(1, 2)
-    hand_over(0, 3)
-    take(0, 1, (2, 3))
-    pre_act(1, PAIR, PAIR)
     hand_over(1, 0)
     load2.wait()
 
@@ -481,13 +484,12 @@
     hand_over(1, 2)
     pieces(1, 0, PAIR)
     add_cores(0, (1, 0))
+    take(1, 0, (2, 3))
+    hidden(0, PAIR, PAIR)
     hand_over(1, 3)
+    pieces(0, PAIR, PAIR)
     take(1, 1, (2, 3))
     hidden(1, PAIR, PAIR)
-    pieces(1, PAIR, PAIR)
-    add_cores(1, (3, 2))
-    take(1, 0, (2, 3))
-    hidden(0, PAIR, PAIR)
 
     def complete(p):
         got(("ps", p))
@@ -508,7 +510,8 @@
 
     got(("ss", 0))
     complete(1)
-    pieces(0, PAIR, PAIR)
+    pieces(1, PAIR, PAIR)
+    add_cores(1, (3, 2))
     complete(OWN)
     got(("ss", 1))
     complete(3)

time: 152 us -> 148 us (0.974)
  the two profiles are of different devices: /device:TPU:29 before, /device:TPU:1 now
where the time goes in v3:
time: 148 us
  Pallas kernels  146 us (99%)
  local copies, waits for them, and re-layouts  1.88 us (1%)
    pallas_call x1, Pallas kernels, tick(): pl.pallas_call(tick_kernel, out_shape=jax.ShapeDtypeStruct((TOK, D), BF),...  146 us

profile of v3, /device:TPU:1, one launch (start us, length us, event | category | flops | bytes accessed | tf_op | source)
XLA Modules:
  0.0 148.1 jit_solution(1754150659972715572)
XLA Ops:
  0.0 146.2 %tick.1 = bf16[128,2048]{1,0:T(8,128)(2,1)} custom-call(bf16[128,4096]{1,0:T(8,128)(2,1)} %bitcast.16, bf16[128,4096]{1,0:T(8,128)(2,1)} %bitcast.17, bf16[128,2048]{1,0:T(8,128)(2,1)} %bitcast.18, bf16[128,2048]{1,0:T(8,128)(2,1)} %bitcast.19, f32[1,2048]{1,0:T(1,128)} %gain.1, s32[2,128]{1,0:T(2,128)} %bitcast.20, f32[2,128]{1,0:T(2,128)} %bitcast.21, ...), custom_call_target="tpu_custom_call" | custom-call | tf_op jit(solution)/shard_map/tick/pallas_call | solution.py:589
  146.3 1.9 %copy.11 = bf16[1,128,2048]{2,1,0:T(8,128)(2,1)} copy(bf16[1,128,2048]{2,1,0:T(8,128)(2,1)} %bitcast.15) | data formatting | bytes 1048576

commit v4 on v3

--- a/solution.py
+++ b/solution.py
@@ -343,10 +343,10 @@
         go(rc(QS.at[p], QR.at[p], q_s.at[p], q_r.at[p], sib), ("swap", p))
         product(c, p, keep_mine)
 
+    send_out(0, 3)
     half_product(0)
     spread(0)
     forward(0, 1)
-    send_out(0, 3)
     for half in range(2):
         for r in range(LANES):
             got(("zk", 1, r, half))

time: 148 us -> 146 us (0.986)
  the two profiles are of different devices: /device:TPU:1 before, /device:TPU:29 now
where the time goes in v4:
time: 146 us; the launch traced here: 144 us
  Pallas kernels  142 us (97%)
  local copies, waits for them, and re-layouts  1.88 us (1%)
    pallas_call x1, Pallas kernels, tick(): pl.pallas_call(tick_kernel, out_shape=jax.ShapeDtypeStruct((TOK, D), BF),...  142 us

profile of v4, /device:TPU:29, one launch (start us, length us, event | category | flops | bytes accessed | tf_op | source)
XLA Modules:
  0.0 144.0 jit_solution(10383962304836365451)
XLA Ops:
  0.0 142.1 %tick.1 = bf16[128,2048]{1,0:T(8,128)(2,1)} custom-call(bf16[128,4096]{1,0:T(8,128)(2,1)} %bitcast.16, bf16[128,4096]{1,0:T(8,128)(2,1)} %bitcast.17, bf16[128,2048]{1,0:T(8,128)(2,1)} %bitcast.18, bf16[128,2048]{1,0:T(8,128)(2,1)} %bitcast.19, f32[1,2048]{1,0:T(1,128)} %gain.1, s32[2,128]{1,0:T(2,128)} %bitcast.20, f32[2,128]{1,0:T(2,128)} %bitcast.21, ...), custom_call_target="tpu_custom_call" | custom-call | tf_op jit(solution)/shard_map/tick/pallas_call | solution.py:589
  142.1 1.9 %copy.11 = bf16[1,128,2048]{2,1,0:T(8,128)(2,1)} copy(bf16[1,128,2048]{2,1,0:T(8,128)(2,1)} %bitcast.15) | data formatting | bytes 1048576
